TPU v7x, 512 devices: a whole 4x8x8 slice. The times are simulated.
512 devices in a mesh: dp: 16 (over z, core), fsdp: 4 (over x), tensor: 8 (over y).
Axes of the slice: x: 4, y: 8, z: 8, core: 2. Of those that a mesh axis runs over, the one named last changes fastest.
Arguments:
- tokens: bfloat16 [16384, 8192], P(('dp', 'fsdp'), 'tensor'), may hold values from -700 to 700
- queries: bfloat16 [16384, 8192], P(('dp', 'fsdp'), 'tensor'), may hold values from -140 to 140
- segment_ids: int32 [128, 128], P(('dp', 'fsdp')), may hold values from 0 to 3, never falling along the last dimension, each value on 1 to 64 neighbouring positions
- gain: float32 [8192], P('tensor'), may hold values from 0.1 to 1.9
- key_value_weight: bfloat16 [8192, 2048], P('tensor', 'fsdp'), may hold values from -0.0625 to 0.0625
- plan: int32 [32], replicated, may hold values from 0 to 31, as said below
Outputs:
- attended: bfloat16 [16384, 8192], P(('dp', 'fsdp'), 'tensor')
Inputs may be any that keep to these rules, and one draw needn't show every extreme that they name: plan is a permutation of 0 to 31; from one dp index to another at most 1 micro-batches go, and in every draw some pair of dp indices carries exactly 1.
All inputs are finite; a program needn't handle non-finite values.
Results may differ from a plain program's by a relative error of at most 0.011.
Values may be sent and summed in bfloat16 or wider, within the bound.
No kernel may reach another device: no remote copies, remote signals or barrier semaphores. Data moves between devices by JAX's collectives and lax.ppermute only.
A program may use at most 64 MiB of HBM per device.

v0:
```python
import jax
import jax.numpy as jnp
from jax import lax
from jax.sharding import PartitionSpec as P

HEAD_SIZE = 128
epsilon = 1e-05


def total_of_pieces(array, axis):
    parts = lax.all_gather(array, axis)
    return parts.sum(axis=0)


def pack_rows(send_index, send_valid, flat_rows, length):
    ranks_here = send_index.shape[0]
    slots_here = send_index.shape[1]
    taken = jnp.take(flat_rows, send_index.reshape(-1), axis=0)
    sent = taken * send_valid.astype(flat_rows.dtype)
    return sent.reshape(ranks_here, slots_here, length, -1)


def unpack_rows(keep_index, arrived):
    flat = arrived.reshape(arrived.shape[0] * arrived.shape[1], -1)
    return jnp.take(flat, keep_index, axis=0)


def project(rows, gain, key_value_weight):
    values = rows.astype(jnp.float32)
    stats = total_of_pieces(jnp.sum(values * values, axis=1), "tensor")
    full_width = rows.shape[1] * lax.axis_size("tensor")
    scale = lax.rsqrt(stats / full_width + epsilon)
    normed = (values * scale[:, None] * gain).astype(jnp.bfloat16)
    partial_value = jnp.dot(
        normed,
        lax.all_gather(key_value_weight, "fsdp", axis=1, tiled=True),
        preferred_element_type=jnp.float32,
    )
    return lax.psum_scatter(partial_value, "tensor", scatter_dimension=1, tiled=True)


def attend(query_row_block, key_value_rows, documents):
    batches, length = documents.shape
    heads_kv = key_value_rows.shape[1] // (2 * HEAD_SIZE)
    head_group = query_row_block.shape[1] // (heads_kv * HEAD_SIZE)
    query_head_count = query_row_block.astype(jnp.float32).reshape(
        batches, length, heads_kv, head_group, HEAD_SIZE
    )
    key_value_heads = key_value_rows.reshape(batches, length, heads_kv, 2, HEAD_SIZE)
    scores = jnp.einsum(
        "mqhgd,mkhd->mhgqk",
        query_head_count,
        key_value_heads[:, :, :, 0],
        precision=lax.Precision.HIGHEST,
    ) * HEAD_SIZE ** (-0.5)
    positions = jnp.arange(length, dtype=jnp.int32)
    causal = positions[:, None] >= positions[None, :]
    allowed = (documents[:, :, None] == documents[:, None, :]) & causal[None]
    scores = jnp.where(allowed[:, None, None], scores, -1e30)
    row_max = jnp.max(scores, axis=-1, keepdims=True)
    expo = jnp.exp(scores - row_max)
    weights = (expo / jnp.sum(expo, axis=-1, keepdims=True)).astype(jnp.bfloat16)
    mixed = jnp.einsum(
        "mhgqk,mkhd->mqhgd",
        weights.astype(jnp.float32),
        key_value_heads[:, :, :, 1],
        precision=lax.Precision.HIGHEST,
    )
    return mixed.reshape(batches * length, -1).astype(jnp.bfloat16)


def shards(tokens, queries, segment_ids, gain, key_value_weight, plan):
    rank_count = lax.axis_size("dp")
    own_rank = lax.axis_index("dp")
    batches = segment_ids.shape[0]
    length = segment_ids.shape[1]
    slot_cap = (batches + rank_count - 1) // rank_count
    dest_rank = plan.reshape(rank_count, batches) // batches
    slot_range = jnp.arange(batches, dtype=jnp.int32)
    same_dest = dest_rank[:, :, None] == dest_rank[:, None, :]
    earlier = slot_range[None, None, :] < slot_range[None, :, None]
    arrival = jnp.sum((same_dest & earlier).astype(jnp.int32), axis=2)
    own_dest = lax.dynamic_index_in_dim(dest_rank, own_rank, 0, keepdims=False)
    own_arrival = lax.dynamic_index_in_dim(arrival, own_rank, 0, keepdims=False)
    rank_range = jnp.arange(rank_count, dtype=jnp.int32)
    cap_range = jnp.arange(slot_cap, dtype=jnp.int32)
    send_hits = (
        (own_dest[None, None, :] == rank_range[:, None, None])
        & (own_arrival[None, None, :] == cap_range[None, :, None])
    ).astype(jnp.int32)
    send_index = jnp.sum(send_hits * slot_range[None, None, :], axis=2)
    send_valid = jnp.sum(send_hits, axis=2)
    inverse = jnp.argsort(plan)
    sources = lax.dynamic_slice_in_dim(inverse, own_rank * batches, batches)
    source_rank = sources // batches
    source_arrival = jnp.take(arrival.reshape(-1), sources)
    keep_index = source_rank * slot_cap + source_arrival
    local_kv = project(tokens, gain, key_value_weight)
    results = attend(queries, local_kv, segment_ids)
    parcel = pack_rows(send_index, send_valid, results.reshape(batches, -1), length)
    arrived = lax.all_to_all(parcel, "dp", split_axis=0, concat_axis=0, tiled=True)
    return unpack_rows(keep_index, arrived).reshape(batches * length, -1)


def solution(mesh):
    placed = (
        P(("dp", "fsdp"), "tensor"),
        P(("dp", "fsdp"), "tensor"),
        P(("dp", "fsdp"), None),
        P("tensor"),
        P("tensor", "fsdp"),
        P(),
    )
    return jax.shard_map(
        shards, mesh=mesh, in_specs=placed, out_specs=P(("dp", "fsdp"), "tensor"), check_vma=False
    )
```

profile of v0, /device:TPU:1, one launch (start us, length us, event | category | flops | bytes accessed | tf_op | source)
XLA Modules:
  0.0 254.4 jit_solution(3766419235261938822)
XLA Ops:
  6.5 0.7 all-gather.4.cloned.1.call-update
  7.3 1.2 fusion.4
  8.5 13.8 %all-gather.1 = f32[8,1,256]{2,1,0:T(1,128)S(1)} all-gather(f32[1,1,256]{2,1,0:T(1,128)S(1)} %bitcast.63), channel_id=2, replica_groups=mesh['dp'=16,'fsdp'=4,'tensor'=8] {'tensor'}, dimensions={0}, use_global_device_ids=true | all-gather | bytes 9216 | tf_op jit(solution)/shard_map/all_gather | solution.py:11
  22.4 46.1 %all-gather.4.cloned.1.call-done = bf16[1024,2048]{1,0:T(8,128)(2,1)} async-done(((bf16[1024,512]{1,0:T(8,128)(2,1)}), bf16[1024,2048]{1,0:T(8,128)(2,1)}) %all-gather.4.cloned.1.call-update) | async-done | bytes 4194320 | tf_op jit(solution)/shard_map/all_gather | solution.py:36
  68.5 5.0 %fusion.8 = f32[256,2048]{1,0:T(8,128)} fusion(bf16[1024,2048]{1,0:T(8,128)(2,1)} %all-gather.4.cloned.1.call-done, bf16[256,1024]{1,0:T(8,128)(2,1)} %param.6, f32[1024]{0:T(1024)} %param.9, f32[256]{0:T(256)S(1)} %add_rsqrt_fusion), kind=kOutput, calls=%fused_computation.21 | convolution fusion | flops 1074790400 | bytes 6820864 | tf_op jit(solution)/shard_map/dot_general | solution.py:34
  74.0 0.2 compare_reduce_fusion
  74.4 0.1 compare_and_fusion
  74.5 40.1 %reduce-scatter.2.cloned.1.call-done = f32[256,256]{1,0:T(8,128)} async-done(((f32[256,2048]{1,0:T(8,128)}), f32[256,256]{1,0:T(8,128)}) %reduce-scatter.2.cloned.1.call-update) | async-done | bytes 262160 | tf_op jit(solution)/shard_map/reduce_scatter | solution.py:39
  114.5 1.1 reshape.341
  115.6 0.2 fusion.21
  115.8 0.7 fusion.22
  116.5 0.2 fusion.7
  116.7 0.6 fusion.3
  117.3 0.3 copy.29
  117.6 0.1 convert_element_type.53
  117.8 0.4 fusion.20
  118.2 1.9 gather_fusion.1
  120.1 3.3 %gather_fusion.2 = bf16[16,65536]{1,0:T(8,128)(2,1)} fusion(bf16[2,65536]{1,0:T(2,128)(2,1)S(1)} %get-tuple-element.14, s32[1024]{0:T(1024)S(1)} %pad_clamp_fusion.1), kind=kCustom, calls=%fused_computation.2 | custom fusion | bytes 4194368 | tf_op jit(solution)/shard_map/jit(_take)/gather | solution.py:18
  123.4 1.9 pad_maximum_fusion
  125.3 2.3 copy.37
  127.6 2.6 %fusion = bf16[16,1,128,1024]{3,2,1,0:T(8,128)(2,1)} fusion(pred[16]{0:T(512)(128)(4,1)S(1)} %compare_and_fusion.1, bf16[16]{0:T(256)(128)(2,1)S(1)} %convert_element_type.55, bf16[2,8,128,1024]{3,2,1,0:T(8,128)(2,1)S(1)} %copy.37), kind=kLoop, calls=%fused_computation.7 | loop fusion | flops 4194304 | bytes 8388656 | tf_op jit(solution)/shard_map/mul | solution.py:19
  130.2 11.9 %all-to-all-start = ((bf16[16,1,128,1024]{3,2,1,0:T(8,128)(2,1)}), bf16[16,1,128,1024]{3,2,1,0:T(8,128)(2,1)}, u32[]{:S(2)}, u32[]{:S(2)}) async-start(bf16[16,1,128,1024]{3,2,1,0:T(8,128)(2,1)} %fusion), calls=%async_computation.1 | async-start | bytes 8388608 | tf_op jit(solution)/shard_map/all_to_all | solution.py:101
  142.2 1.6 sort.17
  144.0 0.6 gather_fusion
  144.8 90.9 %all-to-all-done = bf16[16,1,128,1024]{3,2,1,0:T(8,128)(2,1)} async-done(((bf16[16,1,128,1024]{3,2,1,0:T(8,128)(2,1)}), bf16[16,1,128,1024]{3,2,1,0:T(8,128)(2,1)}, u32[]{:S(2)}, u32[]{:S(2)}) %all-to-all-start) | async-done | bytes 4194336 | tf_op jit(solution)/shard_map/all_to_all | solution.py:101
  235.7 4.5 %copy.38 = bf16[2,8,128,1024]{3,1,2,0:T(8,128)(2,1)S(1)} copy(bf16[2,8,128,1024]{3,2,1,0:T(8,128)(2,1)} %bitcast.36) | data formatting | bytes 8388608
  240.2 1.6 fusion.19
  241.8 3.0 %gather_fusion.3 = bf16[2,65536]{1,0:T(2,128)(2,1)S(1)} fusion(bf16[16,65536]{1,0:T(8,128)(2,1)} %get-tuple-element.11, s32[1024]{0:T(1024)S(1)} %pad_clamp_fusion), kind=kCustom, calls=%fused_computation.3 | custom fusion | bytes 524296 | tf_op jit(solution)/shard_map/jit(_take)/gather | solution.py:25
  244.8 0.9 gather_fusion.4
  245.7 0.5 pad_maximum_fusion.1
  246.2 0.5 gather.20
  246.7 0.9 broadcast_select_fusion
  (32 shorter events, 1.0 us)
Async XLA Ops:
  6.5 62.0 %all-gather.4.cloned.1.call-start = ((), (), s32[]{:S(2)}) async-start(), calls=%async_computation.2 | async-start | bytes 5242880 | tf_op jit(solution)/shard_map/all_gather | solution.py:36
  7.3 107.3 %reduce-scatter.2.cloned.1.call-start = ((), (), s32[]{:S(2)}) async-start(), calls=%async_computation.3 | async-start | bytes 2359296 | tf_op jit(solution)/shard_map/reduce_scatter | solution.py:39
  22.4 51.2 %copy-start.2 = (s32[32]{0:T(128)S(1)}, s32[32]{0:T(128)}, u32[]{:S(2)}) copy-start(s32[32]{0:T(128)} %param.11) | copy-start | bytes 388
  22.4 51.4 %copy-start = (bf16[256,1024]{1,0:T(8,128)(2,1)S(1)}, bf16[256,1024]{1,0:T(8,128)(2,1)}, u32[]{:S(2)}) copy-start(bf16[256,1024]{1,0:T(8,128)(2,1)} %param.7) | copy-start | bytes 1572868
  22.4 51.9 %copy-start.1 = (s32[2,128]{1,0:T(2,128)S(1)}, s32[2,128]{1,0:T(2,128)}, u32[]{:S(2)}) copy-start(s32[2,128]{1,0:T(2,128)} %param.8) | copy-start | bytes 3076
  130.2 105.5 %all-to-all-start = ((bf16[16,1,128,1024]{3,2,1,0:T(8,128)(2,1)}), bf16[16,1,128,1024]{3,2,1,0:T(8,128)(2,1)}, u32[]{:S(2)}, u32[]{:S(2)}) async-start(bf16[16,1,128,1024]{3,2,1,0:T(8,128)(2,1)} %fusion), calls=%async_computation.1 | async-start | bytes 8388608 | tf_op jit(solution)/shard_map/all_to_all | solution.py:101
Sparse Core Ops, SparseCore 0:
  9.5 59.0 all-gather.3
  73.7 40.8 reduce-scatter.1
where the time goes:
time: 255 us; the launch traced here: 254 us
  waiting for transfers between devices  178 us (70%)
  local copies, waits for them, and re-layouts  21.3 us (8%)
  blocking collectives  13.8 us (5%)
  between operations  13.6 us (5%)
  starting transfers between devices  12 us (5%)
  other arithmetic  9.59 us (4%)
  matrix products  6.33 us (2%)
    all_to_all x1, waiting for transfers between devices, shards(): lax.all_to_all(parcel, 'dp', split_axis=0, concat_axis=0, tiled=True)  90.9 us
    all_gather x1, waiting for transfers between devices, project(): lax.all_gather(key_value_weight, 'fsdp', axis=1, tiled=True)  46.1 us
    reduce_scatter x1, waiting for transfers between devices, project(): lax.psum_scatter(partial_value, 'tensor', scatter_dimension=1, tiled=True)  40.1 us
    all_gather x1, blocking collectives, total_of_pieces(): parts = lax.all_gather(array, axis)  13.8 us
    all_to_all x1, starting transfers between devices, shards(): lax.all_to_all(parcel, 'dp', split_axis=0, concat_axis=0, tiled=True)  11.9 us
    unnamed x9, local copies, waits for them, and re-layouts  6.94 us
    gather x4, local copies, waits for them, and re-layouts, unpack_rows(): return jnp.take(flat, keep_index, axis=0)  5.95 us
    gather x3, local copies, waits for them, and re-layouts, pack_rows(): taken = jnp.take(flat_rows, send_index.reshape(-1), axis=0)  5.59 us
  transfers between devices with their start and end apart: 3, of which 3 were waited for; matrix products, arithmetic and copies ran while one was open for 2% of the time, Pallas kernels for 0%

commit v1 on v0

--- a/solution.py
+++ b/solution.py
@@ -5,6 +5,17 @@
 
 HEAD_SIZE = 128
 epsilon = 1e-05
+
+
+def in_blocks(x, dim, size):
+    before, after = (x.shape[:dim], x.shape[dim + 1 :])
+    return jnp.moveaxis(x.reshape(*before, size, -1, *after), dim, 0)
+
+
+def in_order(blocks, dim):
+    dims = list(blocks.shape[1:])
+    dims[dim] *= blocks.shape[0]
+    return jnp.moveaxis(blocks, 0, dim).reshape(dims)
 
 
 def total_of_pieces(array, axis):
@@ -98,7 +109,14 @@
     local_kv = project(tokens, gain, key_value_weight)
     results = attend(queries, local_kv, segment_ids)
     parcel = pack_rows(send_index, send_valid, results.reshape(batches, -1), length)
-    arrived = lax.all_to_all(parcel, "dp", split_axis=0, concat_axis=0, tiled=True)
+    size, index = (lax.axis_size("dp"), lax.axis_index("dp"))
+    parts_2 = in_blocks(parcel, 0, size)
+    finished = [parts_2[index]]
+    for step in range(1, size):
+        sent_2 = parts_2[index ^ step]
+        finished.append(lax.ppermute(sent_2, "dp", [(i, i ^ step) for i in range(size)]))
+    parts_2 = jnp.stack(finished)[index ^ jnp.arange(size)]
+    arrived = in_order(parts_2, 0)
     return unpack_rows(keep_index, arrived).reshape(batches * length, -1)
 
 

time: 255 us -> 309 us (1.21)
  starting transfers between devices: 12 us -> 98.9 us
  waiting for transfers between devices: 178 us -> 129 us
  local copies, waits for them, and re-layouts: 21.3 us -> 38.4 us
    ppermute x0 -> x15, starting transfers between devices: none -> 98.8 us  [shards(): lax.ppermute(sent_2, 'dp', [(i, i ^ step) for i in range(size)])]
    all_to_all x1 -> x0, waiting for transfers between devices: 90.9 us -> none  [shards(): lax.all_to_all(parcel, 'dp', split_axis=0, concat_axis=0, tiled=True)]
    ppermute x0 -> x15, waiting for transfers between devices: none -> 44.9 us  [shards(): lax.ppermute(sent_2, 'dp', [(i, i ^ step) for i in range(size)])]
    all_to_all x1 -> x0, starting transfers between devices: 11.9 us -> none  [shards(): lax.all_to_all(parcel, 'dp', split_axis=0, concat_axis=0, tiled=True)]
    unnamed x9 -> x23, local copies, waits for them, and re-layouts: 6.94 us -> 17.1 us
    gather x0 -> x1, local copies, waits for them, and re-layouts: none -> 4.97 us  [shards(): parts_2 = jnp.stack(finished)[index ^ jnp.arange(size)]]
  transfers between devices with their start and end apart: 3 -> 17, of which waited for: 3 -> 9; matrix products, arithmetic and copies ran while one was open for 2% -> 5% of each run, Pallas kernels for 0% -> 0%
where the time goes in v1:
time: 309 us; the launch traced here: 308 us
  waiting for transfers between devices  129 us (42%)
  starting transfers between devices  98.9 us (32%)
  local copies, waits for them, and re-layouts  38.4 us (12%)
  blocking collectives  13.8 us (4%)
  between operations  13.8 us (4%)
  other arithmetic  7.43 us (2%)
  matrix products  6.33 us (2%)
    ppermute x15, starting transfers between devices, shards(): lax.ppermute(sent_2, 'dp', [(i, i ^ step) for i in range(size)])  98.8 us
    all_gather x1, waiting for transfers between devices, project(): lax.all_gather(key_value_weight, 'fsdp', axis=1, tiled=True)  46.1 us
    ppermute x15, waiting for transfers between devices, shards(): lax.ppermute(sent_2, 'dp', [(i, i ^ step) for i in range(size)])  44.9 us
    reduce_scatter x1, waiting for transfers between devices, project(): lax.psum_scatter(partial_value, 'tensor', scatter_dimension=1, tiled=True)  37.5 us
    unnamed x23, local copies, waits for them, and re-layouts  17.1 us
    all_gather x1, blocking collectives, total_of_pieces(): parts = lax.all_gather(array, axis)  13.8 us
  transfers between devices with their start and end apart: 17, of which 9 were waited for; matrix products, arithmetic and copies ran while one was open for 5% of the time, Pallas kernels for 0%

profile of v1, /device:TPU:1, one launch (start us, length us, event | category | flops | bytes accessed | tf_op | source)
XLA Modules:
  0.0 308.0 jit_solution(8386668431371961148)
XLA Ops:
  8.5 13.8 %all-gather.1 = f32[8,1,256]{2,1,0:T(1,128)S(1)} all-gather(f32[1,1,256]{2,1,0:T(1,128)S(1)} %bitcast.122), channel_id=2, replica_groups=mesh['dp'=16,'fsdp'=4,'tensor'=8] {'tensor'}, dimensions={0}, use_global_device_ids=true | all-gather | bytes 9216 | tf_op jit(solution)/shard_map/all_gather | solution.py:22
  22.4 46.1 %all-gather.4.cloned.1.call-done = bf16[1024,2048]{1,0:T(8,128)(2,1)} async-done(((bf16[1024,512]{1,0:T(8,128)(2,1)}), bf16[1024,2048]{1,0:T(8,128)(2,1)}) %all-gather.4.cloned.1.call-update) | async-done | bytes 4194320 | tf_op jit(solution)/shard_map/all_gather | solution.py:47
  68.5 5.0 %fusion.7 = f32[256,2048]{1,0:T(8,128)} fusion(bf16[1024,2048]{1,0:T(8,128)(2,1)} %all-gather.4.cloned.1.call-done, bf16[256,1024]{1,0:T(8,128)(2,1)} %param.6, f32[1024]{0:T(1024)} %param.9, f32[256]{0:T(256)S(1)} %add_rsqrt_fusion), kind=kOutput, calls=%fused_computation.21 | convolution fusion | flops 1074790400 | bytes 6820864 | tf_op jit(solution)/shard_map/dot_general | solution.py:45
  77.2 37.5 %reduce-scatter.2.cloned.1.call-done = f32[256,256]{1,0:T(8,128)} async-done(((f32[256,2048]{1,0:T(8,128)}), f32[256,256]{1,0:T(8,128)}) %reduce-scatter.2.cloned.1.call-update) | async-done | bytes 262160 | tf_op jit(solution)/shard_map/reduce_scatter | solution.py:50
  118.3 1.9 gather_fusion.2
  120.2 3.3 %gather_fusion.3 = bf16[16,65536]{1,0:T(8,128)(2,1)} fusion(bf16[2,65536]{1,0:T(2,128)(2,1)S(1)} %get-tuple-element.30, s32[1024]{0:T(1024)S(1)} %get-tuple-element.36), kind=kCustom, calls=%fused_computation.3 | custom fusion | bytes 4194368 | tf_op jit(solution)/shard_map/jit(_take)/gather | solution.py:29
  123.5 1.9 pad_maximum_fusion
  125.4 2.3 copy.35
  129.4 6.4 %collective-permute-start = (bf16[1,1,128,1024]{3,2,1,0:T(8,128)(2,1)S(1)}, bf16[1,1,128,1024]{3,2,1,0:T(8,128)(2,1)S(1)}, u32[]{:S(2)}, u32[]{:S(2)}) collective-permute-start(bf16[1,1,128,1024]{3,2,1,0:T(8,128)(2,1)S(1)} %get-tuple-element.27), channel_id=1, source_target_pairs={{0,32},{32,0},{64,96},{96,64},{128,160},{160,128},{192,224},{224,1... | collective-permute-start | bytes 786440 | tf_op jit(solution)/shard_map/ppermute | solution.py:117
  135.8 3.6 %collective-permute-start.1 = (bf16[1,1,128,1024]{3,2,1,0:T(8,128)(2,1)S(1)}, bf16[1,1,128,1024]{3,2,1,0:T(8,128)(2,1)S(1)}, u32[]{:S(2)}, u32[]{:S(2)}) collective-permute-start(bf16[1,1,128,1024]{3,2,1,0:T(8,128)(2,1)S(1)} %get-tuple-element.26), channel_id=1, source_target_pairs={{0,64},{32,96},{64,0},{96,32},{128,192},{160,224},{192,128},{224,1... | collective-permute-start | bytes 786440 | tf_op jit(solution)/shard_map/ppermute | solution.py:117
  139.4 1.9 collective-permute-start.2
  141.4 4.6 %collective-permute-start.3 = (bf16[1,1,128,1024]{3,2,1,0:T(8,128)(2,1)S(1)}, bf16[1,1,128,1024]{3,2,1,0:T(8,128)(2,1)S(1)}, u32[]{:S(2)}, u32[]{:S(2)}) collective-permute-start(bf16[1,1,128,1024]{3,2,1,0:T(8,128)(2,1)S(1)} %get-tuple-element.24), channel_id=1, source_target_pairs={{0,128},{32,160},{64,192},{96,224},{128,0},{160,32},{192,64},{224,... | collective-permute-start | bytes 786440 | tf_op jit(solution)/shard_map/ppermute | solution.py:117
  146.0 2.1 collective-permute-start.4
  148.1 5.2 %collective-permute-start.5 = (bf16[1,1,128,1024]{3,2,1,0:T(8,128)(2,1)S(1)}, bf16[1,1,128,1024]{3,2,1,0:T(8,128)(2,1)S(1)}, u32[]{:S(2)}, u32[]{:S(2)}) collective-permute-start(bf16[1,1,128,1024]{3,2,1,0:T(8,128)(2,1)S(1)} %get-tuple-element.22), channel_id=1, source_target_pairs={{0,192},{32,224},{64,128},{96,160},{128,64},{160,96},{192,0},{224,... | collective-permute-start | bytes 786440 | tf_op jit(solution)/shard_map/ppermute | solution.py:117
  154.1 2.3 collective-permute-start.6
  158.9 5.6 %collective-permute-start.7 = (bf16[1,1,128,1024]{3,2,1,0:T(8,128)(2,1)S(1)}, bf16[1,1,128,1024]{3,2,1,0:T(8,128)(2,1)S(1)}, u32[]{:S(2)}, u32[]{:S(2)}) collective-permute-start(bf16[1,1,128,1024]{3,2,1,0:T(8,128)(2,1)S(1)} %get-tuple-element.20), channel_id=1, source_target_pairs={{0,256},{32,288},{64,320},{96,352},{128,384},{160,416},{192,448},{... | collective-permute-start | bytes 786440 | tf_op jit(solution)/shard_map/ppermute | solution.py:117
  165.2 32.5 %collective-permute-start.8 = (bf16[1,1,128,1024]{3,2,1,0:T(8,128)(2,1)S(1)}, bf16[1,1,128,1024]{3,2,1,0:T(8,128)(2,1)S(1)}, u32[]{:S(2)}, u32[]{:S(2)}) collective-permute-start(bf16[1,1,128,1024]{3,2,1,0:T(8,128)(2,1)S(1)} %get-tuple-element.19), channel_id=1, source_target_pairs={{0,288},{32,256},{64,352},{96,320},{128,416},{160,384},{192,480},{... | collective-permute-start | bytes 786440 | tf_op jit(solution)/shard_map/ppermute | solution.py:117
  198.5 3.0 collective-permute-done.4
  201.5 1.9 collective-permute-start.9
  204.1 18.0 %collective-permute-start.10 = (bf16[1,1,128,1024]{3,2,1,0:T(8,128)(2,1)S(1)}, bf16[1,1,128,1024]{3,2,1,0:T(8,128)(2,1)S(1)}, u32[]{:S(2)}, u32[]{:S(2)}) collective-permute-start(bf16[1,1,128,1024]{3,2,1,0:T(8,128)(2,1)S(1)} %get-tuple-element.17), channel_id=1, source_target_pairs={{0,352},{32,320},{64,288},{96,256},{128,480},{160,448},{192,416},{... | collective-permute-start | bytes 786440 | tf_op jit(solution)/shard_map/ppermute | solution.py:117
  222.9 3.0 collective-permute-start.11
  226.6 3.4 %collective-permute-start.12 = (bf16[1,1,128,1024]{3,2,1,0:T(8,128)(2,1)S(1)}, bf16[1,1,128,1024]{3,2,1,0:T(8,128)(2,1)S(1)}, u32[]{:S(2)}, u32[]{:S(2)}) collective-permute-start(bf16[1,1,128,1024]{3,2,1,0:T(8,128)(2,1)S(1)} %get-tuple-element.15), channel_id=1, source_target_pairs={{0,416},{32,384},{64,480},{96,448},{128,288},{160,256},{192,352},{... | collective-permute-start | bytes 786440 | tf_op jit(solution)/shard_map/ppermute | solution.py:117
  230.8 2.1 collective-permute-start.13
  233.6 6.1 %collective-permute-start.14 = (bf16[1,1,128,1024]{3,2,1,0:T(8,128)(2,1)S(1)}, bf16[1,1,128,1024]{3,2,1,0:T(8,128)(2,1)S(1)}, u32[]{:S(2)}, u32[]{:S(2)}) collective-permute-start(bf16[1,1,128,1024]{3,2,1,0:T(8,128)(2,1)S(1)} %get-tuple-element.13), channel_id=1, source_target_pairs={{0,480},{32,448},{64,416},{96,384},{128,352},{160,320},{192,288},{... | collective-permute-start | bytes 786440 | tf_op jit(solution)/shard_map/ppermute | solution.py:117
  240.4 19.5 %collective-permute-done.10 = bf16[1,1,128,1024]{3,2,1,0:T(8,128)(2,1)S(1)} collective-permute-done((bf16[1,1,128,1024]{3,2,1,0:T(8,128)(2,1)S(1)}, bf16[1,1,128,1024]{3,2,1,0:T(8,128)(2,1)S(1)}, u32[]{:S(2)}, u32[]{:S(2)}) %collective-permute-start.10) | collective-permute-done | bytes 262176 | tf_op jit(solution)/shard_map/ppermute | solution.py:117
  260.6 4.9 %collective-permute-done.11 = bf16[1,1,128,1024]{3,2,1,0:T(8,128)(2,1)S(1)} collective-permute-done((bf16[1,1,128,1024]{3,2,1,0:T(8,128)(2,1)S(1)}, bf16[1,1,128,1024]{3,2,1,0:T(8,128)(2,1)S(1)}, u32[]{:S(2)}, u32[]{:S(2)}) %collective-permute-start.11) | collective-permute-done | bytes 262176 | tf_op jit(solution)/shard_map/ppermute | solution.py:117
  266.2 4.9 %collective-permute-done.12 = bf16[1,1,128,1024]{3,2,1,0:T(8,128)(2,1)S(1)} collective-permute-done((bf16[1,1,128,1024]{3,2,1,0:T(8,128)(2,1)S(1)}, bf16[1,1,128,1024]{3,2,1,0:T(8,128)(2,1)S(1)}, u32[]{:S(2)}, u32[]{:S(2)}) %collective-permute-start.12) | collective-permute-done | bytes 262176 | tf_op jit(solution)/shard_map/ppermute | solution.py:117
  271.8 7.1 %collective-permute-done.13 = bf16[1,1,128,1024]{3,2,1,0:T(8,128)(2,1)S(1)} collective-permute-done((bf16[1,1,128,1024]{3,2,1,0:T(8,128)(2,1)S(1)}, bf16[1,1,128,1024]{3,2,1,0:T(8,128)(2,1)S(1)}, u32[]{:S(2)}, u32[]{:S(2)}) %collective-permute-start.13) | collective-permute-done | bytes 262176 | tf_op jit(solution)/shard_map/ppermute | solution.py:117
  279.6 4.0 %collective-permute-done.14 = bf16[1,1,128,1024]{3,2,1,0:T(8,128)(2,1)S(1)} collective-permute-done((bf16[1,1,128,1024]{3,2,1,0:T(8,128)(2,1)S(1)}, bf16[1,1,128,1024]{3,2,1,0:T(8,128)(2,1)S(1)}, u32[]{:S(2)}, u32[]{:S(2)}) %collective-permute-start.14) | collective-permute-done | bytes 262176 | tf_op jit(solution)/shard_map/ppermute | solution.py:117
  284.3 5.0 %gather_fusion.1 = bf16[16,128,1024]{2,1,0:T(8,128)(2,1)} fusion(bf16[16,128,1024]{2,1,0:T(8,128)(2,1)} %bitcast.46, s32[1024]{0:T(1024)S(1)} %pad_clamp_fusion.1), kind=kCustom, calls=%fused_computation.1 | custom fusion | bytes 8388672 | tf_op jit(solution)/shard_map/gather | solution.py:118
  289.3 4.5 %copy.36 = bf16[2,8,128,1024]{3,1,2,0:T(8,128)(2,1)S(1)} copy(bf16[2,8,128,1024]{3,2,1,0:T(8,128)(2,1)} %bitcast.117) | data formatting | bytes 8388608
  295.4 3.0 gather_fusion.4
  (78 shorter events, 27.7 us)
Async XLA Ops:
  6.5 62.0 %all-gather.4.cloned.1.call-start = ((), (), s32[]{:S(2)}) async-start(), calls=%async_computation.1 | async-start | bytes 5242880 | tf_op jit(solution)/shard_map/all_gather | solution.py:47
  7.3 107.4 %reduce-scatter.2.cloned.1.call-start = ((), (), s32[]{:S(2)}) async-start(), calls=%async_computation.2 | async-start | bytes 2359296 | tf_op jit(solution)/shard_map/reduce_scatter | solution.py:50
  22.4 51.3 %copy-start.2 = (s32[32]{0:T(128)S(1)}, s32[32]{0:T(128)}, u32[]{:S(2)}) copy-start(s32[32]{0:T(128)} %param.11) | copy-start | bytes 388
  22.4 53.3 %copy-start = (bf16[256,1024]{1,0:T(8,128)(2,1)S(1)}, bf16[256,1024]{1,0:T(8,128)(2,1)}, u32[]{:S(2)}) copy-start(bf16[256,1024]{1,0:T(8,128)(2,1)} %param.7) | copy-start | bytes 1572868
  22.4 54.6 %copy-start.1 = (s32[2,128]{1,0:T(2,128)S(1)}, s32[2,128]{1,0:T(2,128)}, u32[]{:S(2)}) copy-start(s32[2,128]{1,0:T(2,128)} %param.8) | copy-start | bytes 3076
  129.4 18.8 %collective-permute-start = (bf16[1,1,128,1024]{3,2,1,0:T(8,128)(2,1)S(1)}, bf16[1,1,128,1024]{3,2,1,0:T(8,128)(2,1)S(1)}, u32[]{:S(2)}, u32[]{:S(2)}) collective-permute-start(bf16[1,1,128,1024]{3,2,1,0:T(8,128)(2,1)S(1)} %get-tuple-element.27), channel_id=1, source_target_pairs={{0,32},{32,0},{64,96},{96,64},{128,160},{160,128},{192,224},{224,1... | collective-permute-start | bytes 786440 | tf_op jit(solution)/shard_map/ppermute | solution.py:117
  135.8 18.3 %collective-permute-start.1 = (bf16[1,1,128,1024]{3,2,1,0:T(8,128)(2,1)S(1)}, bf16[1,1,128,1024]{3,2,1,0:T(8,128)(2,1)S(1)}, u32[]{:S(2)}, u32[]{:S(2)}) collective-permute-start(bf16[1,1,128,1024]{3,2,1,0:T(8,128)(2,1)S(1)} %get-tuple-element.26), channel_id=1, source_target_pairs={{0,64},{32,96},{64,0},{96,32},{128,192},{160,224},{192,128},{224,1... | collective-permute-start | bytes 786440 | tf_op jit(solution)/shard_map/ppermute | solution.py:117
  139.4 19.4 %collective-permute-start.2 = (bf16[1,1,128,1024]{3,2,1,0:T(8,128)(2,1)S(1)}, bf16[1,1,128,1024]{3,2,1,0:T(8,128)(2,1)S(1)}, u32[]{:S(2)}, u32[]{:S(2)}) collective-permute-start(bf16[1,1,128,1024]{3,2,1,0:T(8,128)(2,1)S(1)} %get-tuple-element.25), channel_id=1, source_target_pairs={{0,96},{32,64},{64,32},{96,0},{128,224},{160,192},{192,160},{224,1... | collective-permute-start | bytes 786440 | tf_op jit(solution)/shard_map/ppermute | solution.py:117
  141.4 23.9 %collective-permute-start.3 = (bf16[1,1,128,1024]{3,2,1,0:T(8,128)(2,1)S(1)}, bf16[1,1,128,1024]{3,2,1,0:T(8,128)(2,1)S(1)}, u32[]{:S(2)}, u32[]{:S(2)}) collective-permute-start(bf16[1,1,128,1024]{3,2,1,0:T(8,128)(2,1)S(1)} %get-tuple-element.24), channel_id=1, source_target_pairs={{0,128},{32,160},{64,192},{96,224},{128,0},{160,32},{192,64},{224,... | collective-permute-start | bytes 786440 | tf_op jit(solution)/shard_map/ppermute | solution.py:117
  146.0 55.5 %collective-permute-start.4 = (bf16[1,1,128,1024]{3,2,1,0:T(8,128)(2,1)S(1)}, bf16[1,1,128,1024]{3,2,1,0:T(8,128)(2,1)S(1)}, u32[]{:S(2)}, u32[]{:S(2)}) collective-permute-start(bf16[1,1,128,1024]{3,2,1,0:T(8,128)(2,1)S(1)} %get-tuple-element.23), channel_id=1, source_target_pairs={{0,160},{32,128},{64,224},{96,192},{128,32},{160,0},{192,96},{224,... | collective-permute-start | bytes 786440 | tf_op jit(solution)/shard_map/ppermute | solution.py:117
  148.1 56.0 %collective-permute-start.5 = (bf16[1,1,128,1024]{3,2,1,0:T(8,128)(2,1)S(1)}, bf16[1,1,128,1024]{3,2,1,0:T(8,128)(2,1)S(1)}, u32[]{:S(2)}, u32[]{:S(2)}) collective-permute-start(bf16[1,1,128,1024]{3,2,1,0:T(8,128)(2,1)S(1)} %get-tuple-element.22), channel_id=1, source_target_pairs={{0,192},{32,224},{64,128},{96,160},{128,64},{160,96},{192,0},{224,... | collective-permute-start | bytes 786440 | tf_op jit(solution)/shard_map/ppermute | solution.py:117
  154.1 68.8 %collective-permute-start.6 = (bf16[1,1,128,1024]{3,2,1,0:T(8,128)(2,1)S(1)}, bf16[1,1,128,1024]{3,2,1,0:T(8,128)(2,1)S(1)}, u32[]{:S(2)}, u32[]{:S(2)}) collective-permute-start(bf16[1,1,128,1024]{3,2,1,0:T(8,128)(2,1)S(1)} %get-tuple-element.21), channel_id=1, source_target_pairs={{0,224},{32,192},{64,160},{96,128},{128,96},{160,64},{192,32},{224... | collective-permute-start | bytes 786440 | tf_op jit(solution)/shard_map/ppermute | solution.py:117
  158.9 67.7 %collective-permute-start.7 = (bf16[1,1,128,1024]{3,2,1,0:T(8,128)(2,1)S(1)}, bf16[1,1,128,1024]{3,2,1,0:T(8,128)(2,1)S(1)}, u32[]{:S(2)}, u32[]{:S(2)}) collective-permute-start(bf16[1,1,128,1024]{3,2,1,0:T(8,128)(2,1)S(1)} %get-tuple-element.20), channel_id=1, source_target_pairs={{0,256},{32,288},{64,320},{96,352},{128,384},{160,416},{192,448},{... | collective-permute-start | bytes 786440 | tf_op jit(solution)/shard_map/ppermute | solution.py:117
  165.2 65.5 %collective-permute-start.8 = (bf16[1,1,128,1024]{3,2,1,0:T(8,128)(2,1)S(1)}, bf16[1,1,128,1024]{3,2,1,0:T(8,128)(2,1)S(1)}, u32[]{:S(2)}, u32[]{:S(2)}) collective-permute-start(bf16[1,1,128,1024]{3,2,1,0:T(8,128)(2,1)S(1)} %get-tuple-element.19), channel_id=1, source_target_pairs={{0,288},{32,256},{64,352},{96,320},{128,416},{160,384},{192,480},{... | collective-permute-start | bytes 786440 | tf_op jit(solution)/shard_map/ppermute | solution.py:117
  201.5 32.1 %collective-permute-start.9 = (bf16[1,1,128,1024]{3,2,1,0:T(8,128)(2,1)S(1)}, bf16[1,1,128,1024]{3,2,1,0:T(8,128)(2,1)S(1)}, u32[]{:S(2)}, u32[]{:S(2)}) collective-permute-start(bf16[1,1,128,1024]{3,2,1,0:T(8,128)(2,1)S(1)} %get-tuple-element.18), channel_id=1, source_target_pairs={{0,320},{32,352},{64,256},{96,288},{128,448},{160,480},{192,384},{... | collective-permute-start | bytes 786440 | tf_op jit(solution)/shard_map/ppermute | solution.py:117
  204.1 55.8 %collective-permute-start.10 = (bf16[1,1,128,1024]{3,2,1,0:T(8,128)(2,1)S(1)}, bf16[1,1,128,1024]{3,2,1,0:T(8,128)(2,1)S(1)}, u32[]{:S(2)}, u32[]{:S(2)}) collective-permute-start(bf16[1,1,128,1024]{3,2,1,0:T(8,128)(2,1)S(1)} %get-tuple-element.17), channel_id=1, source_target_pairs={{0,352},{32,320},{64,288},{96,256},{128,480},{160,448},{192,416},{... | collective-permute-start | bytes 786440 | tf_op jit(solution)/shard_map/ppermute | solution.py:117
  222.9 42.6 %collective-permute-start.11 = (bf16[1,1,128,1024]{3,2,1,0:T(8,128)(2,1)S(1)}, bf16[1,1,128,1024]{3,2,1,0:T(8,128)(2,1)S(1)}, u32[]{:S(2)}, u32[]{:S(2)}) collective-permute-start(bf16[1,1,128,1024]{3,2,1,0:T(8,128)(2,1)S(1)} %get-tuple-element.16), channel_id=1, source_target_pairs={{0,384},{32,416},{64,448},{96,480},{128,256},{160,288},{192,320},{... | collective-permute-start | bytes 786440 | tf_op jit(solution)/shard_map/ppermute | solution.py:117
  226.6 44.5 %collective-permute-start.12 = (bf16[1,1,128,1024]{3,2,1,0:T(8,128)(2,1)S(1)}, bf16[1,1,128,1024]{3,2,1,0:T(8,128)(2,1)S(1)}, u32[]{:S(2)}, u32[]{:S(2)}) collective-permute-start(bf16[1,1,128,1024]{3,2,1,0:T(8,128)(2,1)S(1)} %get-tuple-element.15), channel_id=1, source_target_pairs={{0,416},{32,384},{64,480},{96,448},{128,288},{160,256},{192,352},{... | collective-permute-start | bytes 786440 | tf_op jit(solution)/shard_map/ppermute | solution.py:117
  230.8 48.1 %collective-permute-start.13 = (bf16[1,1,128,1024]{3,2,1,0:T(8,128)(2,1)S(1)}, bf16[1,1,128,1024]{3,2,1,0:T(8,128)(2,1)S(1)}, u32[]{:S(2)}, u32[]{:S(2)}) collective-permute-start(bf16[1,1,128,1024]{3,2,1,0:T(8,128)(2,1)S(1)} %get-tuple-element.14), channel_id=1, source_target_pairs={{0,448},{32,480},{64,384},{96,416},{128,320},{160,352},{192,256},{... | collective-permute-start | bytes 786440 | tf_op jit(solution)/shard_map/ppermute | solution.py:117
  233.6 50.0 %collective-permute-start.14 = (bf16[1,1,128,1024]{3,2,1,0:T(8,128)(2,1)S(1)}, bf16[1,1,128,1024]{3,2,1,0:T(8,128)(2,1)S(1)}, u32[]{:S(2)}, u32[]{:S(2)}) collective-permute-start(bf16[1,1,128,1024]{3,2,1,0:T(8,128)(2,1)S(1)} %get-tuple-element.13), channel_id=1, source_target_pairs={{0,480},{32,448},{64,416},{96,384},{128,352},{160,320},{192,288},{... | collective-permute-start | bytes 786440 | tf_op jit(solution)/shard_map/ppermute | solution.py:117
Sparse Core Ops, SparseCore 0:
  9.5 59.0 all-gather.3
  73.7 40.9 reduce-scatter.1
